TPU v7x, 32 devices: a whole 2x2x4 slice. The times are simulated.
32 devices in a mesh: groups: 2 (over y), seq: 4 (over z), ffn: 2 (over x), row: 2 (over core).
Axes of the slice: x: 2, y: 2, z: 4, core: 2. Of those that a mesh axis runs over, the one named last changes fastest.
Arguments:
- hidden: bfloat16 [4, 2048, 14336], P(('groups', 'row'), 'seq', 'ffn'), parts along dimension 0, may hold values from -6 to 6
- out_grads: bfloat16 [4, 2048, 4096], P(('groups', 'row'), 'seq', 'ffn'), parts along dimension 0, may hold values from -6 to 6
- proj_in: bfloat16 [14336, 64], P('ffn'), may hold values from -0.046875 to 0.046875
- proj_out: bfloat16 [4096, 64], P('ffn'), may hold values from -0.09375 to 0.09375
- doc_lengths: int32 [4, 16], P(('groups', 'row')), parts along dimension 0, may hold values from 1 to 1024, 2048 in all within a row
Outputs:
- doc_grads: float32 [4, 16, 4096], P(('groups', 'row'), 'seq', 'ffn'), parts along dimension 0
- gram: float32 [8192, 4096], P(('groups', 'seq'), 'ffn'), parts along dimension 0
There are 2 independent parts, one for each index of `groups`. A program takes and returns all parts, laid end to end along the dimension named above; an argument that names none is the same for every part. Nothing has to cross between parts.
Inputs may be any that keep to these rules, and one draw needn't show every extreme that they name: `doc_lengths`: the lengths of each packed row sum to 2048, and the longest of each row is 1024.
All inputs are finite; a program needn't handle non-finite values.
Results may differ from a plain program's by a relative error of at most 0.0003.
Values sent between devices are 32-bit elements; how exact they have to be, the bound alone decides.
A program may use at most 128 MiB of HBM per device.

v0:
```python
import jax
import jax.numpy as jnp
from jax import lax
from jax.sharding import PartitionSpec as P


def doc_matrix(lengths_row, first, count):
    ends = jnp.cumsum(lengths_row)
    starts = ends - lengths_row
    position = first + jnp.arange(count, dtype=jnp.int32)
    inside = (position[None, :] >= starts[:, None]) & (position[None, :] < ends[:, None])
    return inside.astype(jnp.float32)


def local(hidden, out_grads, proj_in, proj_out, doc_lengths):
    tokens_here = hidden.shape[1]
    rank_full = proj_in.shape[1]
    width_share = rank_full // lax.axis_size("ffn")
    seq_index = lax.axis_index("seq")
    ffn_index = lax.axis_index("ffn")
    input_part = jnp.dot(hidden[0], proj_in, preferred_element_type=jnp.float32)
    output_part = jnp.dot(out_grads[0], proj_out, preferred_element_type=jnp.float32)
    input_proj = lax.psum(input_part, "ffn")
    output_piece = lax.psum_scatter(output_part, "ffn", scatter_dimension=1, tiled=True)
    outer = (output_piece[:, :, None] * input_proj[:, None, :]).reshape(
        tokens_here, width_share * rank_full
    )
    lengths_row = doc_lengths[0]
    member = doc_matrix(lengths_row, seq_index * tokens_here, tokens_here)
    partial_docs = jnp.dot(member, outer, precision=lax.Precision.HIGHEST)
    scale = lax.rsqrt(lengths_row.astype(jnp.float32))
    docs_total = doc_lengths.shape[1]
    doc_share = docs_total // lax.axis_size("seq")
    tile_rows = rank_full * rank_full // lax.axis_size("seq")
    tile_cols = width_share * rank_full
    owned = lax.psum_scatter(partial_docs, "seq", scatter_dimension=0, tiled=True)
    own_scale = lax.dynamic_slice_in_dim(scale, seq_index * doc_share, doc_share, 0)
    own_docs = owned * own_scale[:, None]
    widened = lax.all_gather(own_docs, "ffn", axis=1, tiled=True)
    piece = lax.all_gather(widened, ("seq", "row"), axis=0, tiled=True)
    left_part = lax.dynamic_slice_in_dim(piece, seq_index * tile_rows, tile_rows, 1)
    right_part = lax.dynamic_slice_in_dim(piece, ffn_index * tile_cols, tile_cols, 1)
    tile = jnp.einsum("dk,dl->kl", left_part, right_part, precision=lax.Precision.HIGHEST)
    gram = tile / (lax.axis_size("row") * docs_total)
    return (own_docs[None], gram)


def solution(mesh):
    placed = (
        P(("groups", "row"), "seq", "ffn"),
        P(("groups", "row"), "seq", "ffn"),
        P("ffn", None),
        P("ffn", None),
        P(("groups", "row"), None),
    )
    return jax.shard_map(
        local,
        mesh=mesh,
        in_specs=placed,
        out_specs=(P(("groups", "row"), "seq", "ffn"), P(("groups", "seq"), "ffn")),
        check_vma=False,
    )
```

profile of v0, /device:TPU:1, one launch (start us, length us, event | category | flops | bytes accessed | tf_op | source)
XLA Modules:
  0.0 126.8 jit_solution(8047493876493441142)
XLA Ops:
  7.2 0.0 copy-start
  7.2 0.0 copy-start.3
  7.2 0.0 copy-start.1
  7.2 0.0 copy-start.2
  7.2 0.0 all-reduce.4.cloned.1.call-start
  7.3 6.4 %fusion = f32[512,64]{0,1:T(8,128)} fusion(bf16[7168,64]{0,1:T(8,128)(2,1)} %param.7, bf16[1,512,7168]{2,1,0:T(8,128)(2,1)} %param.5), kind=kOutput, calls=%fused_computation | convolution fusion | flops 469762048 | bytes 8388608 | tf_op jit(solution)/shard_map/dot_general | solution.py:21
  13.7 0.0 all-reduce.4.cloned.1.call-update
  13.7 0.0 reduce-scatter.2.cloned.1.call-start
  13.8 0.0 copy-done
  13.8 0.0 copy-done.1
  13.8 1.4 %fusion.2 = f32[512,64]{0,1:T(8,128)} fusion(bf16[2048,64]{0,1:T(8,128)(2,1)S(1)} %copy-done.1, bf16[1,512,2048]{2,1,0:T(8,128)(2,1)S(1)} %copy-done), kind=kOutput, calls=%fused_computation.3 | convolution fusion | flops 134217728 | bytes 2490368 | tf_op jit(solution)/shard_map/dot_general | solution.py:22
  15.2 0.0 reduce-scatter.2.cloned.1.call-update
  15.2 0.0 all-reduce.6.cloned.1.call-start
  15.3 0.0 copy-done.2
  15.3 0.1 copy.11
  15.4 0.1 reduce
  15.5 0.0 copy-done.3
  15.6 0.6 dynamic-slice
  16.8 20.1 %all-reduce.4.cloned.1.call-done = f32[512,64]{0,1:T(8,128)} async-done(((f32[512,64]{0,1:T(8,128)}), f32[512,64]{0,1:T(8,128)}) %all-reduce.4.cloned.1.call-update) | async-done | bytes 131088 | tf_op jit(solution)/shard_map/psum | solution.py:23
  36.9 12.9 %reduce-scatter.2.cloned.1.call-done = f32[512,32]{0,1:T(8,128)} async-done(((f32[512,64]{0,1:T(8,128)}), f32[512,32]{0,1:T(8,128)}) %reduce-scatter.2.cloned.1.call-update) | async-done | bytes 65552 | tf_op jit(solution)/shard_map/reduce_scatter | solution.py:24
  49.8 1.4 %broadcast_multiply_fusion = f32[512,32,64]{0,2,1:T(8,128)S(1)} fusion(f32[512,64]{0,1:T(8,128)} %all-reduce.4.cloned.1.call-done, f32[512,32]{0,1:T(8,128)} %reduce-scatter.2.cloned.1.call-done), kind=kLoop, calls=%fused_computation.5 | loop fusion | flops 1048576 | bytes 4390912 | tf_op jit(solution)/shard_map/mul | solution.py:25
  51.2 2.6 %fusion.6 = f32[16,2048]{1,0:T(8,128)} fusion(f32[512,2048]{0,1:T(8,128)S(1)} %bitcast.20, s32[512]{0:T(512)S(1)} %iota_add_fusion, s32[16]{0:T(128)S(1)} %reduce, s32[16]{0:T(128)S(1)} %bitcast_subtract_fusion), kind=kOutput, calls=%fused_computation.9 | convolution fusion | flops 201351168 | bytes 4327552 | tf_op jit(solution)/shard_map/dot_general | solution.py:30
  53.9 0.0 all-reduce.6.cloned.1.call-update
  53.9 0.1 dynamic_slice.9
  54.0 32.5 %all-reduce.6.cloned.1.call-done = f32[16,2048]{1,0:T(8,128)} async-done(((f32[16,2048]{1,0:T(8,128)}), f32[16,2048]{1,0:T(8,128)}) %all-reduce.6.cloned.1.call-update) | async-done | bytes 131088
  86.5 0.9 dynamic-slice_multiply_fusion
  87.4 3.4 %all_gather.6 = f32[4,4096]{1,0:T(4,128)S(1)} all-gather(f32[4,2048]{1,0:T(4,128)S(1)} %dynamic-slice_multiply_fusion), channel_id=1, replica_groups=mesh['groups'=2,'seq'=4,'ffn'=2,'row'=2] {'ffn'}, dimensions={1}, use_global_device_ids=true | all-gather | bytes 98304 | tf_op jit(solution)/shard_map/all_gather | solution.py:39
  90.8 18.8 %all-gather = f32[8,4,4096]{2,1,0:T(4,128)S(1)} all-gather(f32[1,4,4096]{2,1,0:T(4,128)S(1)} %bitcast.21), channel_id=1, replica_groups=mesh['groups'=2,'seq'=4,'ffn'=2,'row'=2] {'seq','row'}, dimensions={0}, use_global_device_ids=true | all-gather | bytes 589824 | tf_op jit(solution)/shard_map/all_gather | solution.py:40
  109.6 0.2 reshape.46
  109.8 9.0 %convolution_multiply_fusion = f32[1024,2048]{1,0:T(8,128)} fusion(f32[32,4096]{1,0:T(8,128)S(1)} %reshape.46, s32[]{:T(128)S(6)} %select_n.11, s32[]{:T(128)S(6)} %select_n.10), kind=kOutput, calls=%fused_computation.2 | convolution fusion | flops 807403520 | bytes 8781832 | tf_op jit(solution)/shard_map/dk,dl->kl/dot_general | solution.py:43
  118.8 1.5 %fusion.18 = f32[1,4,2048]{2,1,0:T(4,128)} fusion(f32[4]{0:T(128)S(1)} %dynamic_slice.9, f32[16,2048]{1,0:T(8,128)} %all-reduce.6.cloned.1.call-done, u32[]{:T(128)S(6)} %multiply.2), kind=kLoop, calls=%fused_computation.21 | loop fusion | flops 8192 | bytes 65556 | tf_op jit(solution)/shard_map/broadcast_in_dim | solution.py:45
  (4 shorter events, 0.0 us)
Async XLA Ops:
  7.2 6.6 %copy-start = (bf16[1,512,2048]{2,1,0:T(8,128)(2,1)S(1)}, bf16[1,512,2048]{2,1,0:T(8,128)(2,1)}, u32[]{:S(2)}) copy-start(bf16[1,512,2048]{2,1,0:T(8,128)(2,1)} %param.6) | copy-start | bytes 6291460
  7.2 8.4 %copy-start.3 = (u32[32]{0:T(128)S(1)}, u32[32]{0:T(128)}, u32[]{:S(2)}) copy-start(u32[32]{0:T(128)} %constant.34) | copy-start | bytes 388
  7.2 6.6 %copy-start.1 = (bf16[2048,64]{0,1:T(8,128)(2,1)S(1)}, bf16[2048,64]{0,1:T(8,128)(2,1)}, u32[]{:S(2)}) copy-start(bf16[2048,64]{0,1:T(8,128)(2,1)} %param.8) | copy-start | bytes 786436
  7.2 8.1 %copy-start.2 = (s32[1,16]{1,0:T(1,128)S(1)}, s32[1,16]{1,0:T(1,128)}, u32[]{:S(2)}) copy-start(s32[1,16]{1,0:T(1,128)} %param.9) | copy-start | bytes 196
  7.2 29.7 %all-reduce.4.cloned.1.call-start = ((), (), s32[]{:S(2)}) async-start(), calls=%async_computation.2 | async-start | bytes 262144 | tf_op jit(solution)/shard_map/psum | solution.py:23
  13.7 36.1 %reduce-scatter.2.cloned.1.call-start = ((), (), s32[]{:S(2)}) async-start(), calls=%async_computation.1 | async-start | bytes 196608 | tf_op jit(solution)/shard_map/reduce_scatter | solution.py:24
  15.2 71.3 %all-reduce.6.cloned.1.call-start = ((), (), s32[]{:S(2)}) async-start(), calls=%async_computation.3 | async-start | bytes 262144
Sparse Core Ops, SparseCore 0:
  13.8 23.0 all-reduce.3
  39.1 10.6 reduce-scatter.1
  54.0 32.3 all-reduce.5
where the time goes:
time: 127 us
  waiting for transfers between devices  65.5 us (52%)
  blocking collectives  22.2 us (17%)
  matrix products  19.5 us (15%)
  between operations  14.5 us (11%)
  other arithmetic  4.03 us (3%)
    unnamed x4, waiting for transfers between devices  32.5 us
    psum x1, waiting for transfers between devices, local(): input_proj = lax.psum(input_part, 'ffn')  20.1 us
    all_gather x1, blocking collectives, local(): piece = lax.all_gather(widened, ('seq', 'row'), axis=0, tiled=True)  18.8 us
    reduce_scatter x1, waiting for transfers between devices, local(): lax.psum_scatter(output_part, 'ffn', scatter_dimension=1, tiled=True)  12.9 us
    dot_general x1, matrix products, local(): jnp.einsum('dk,dl->kl', left_part, right_part, precision=lax.Precision.HI...  9.01 us
    dot_general x1, matrix products, local(): input_part = jnp.dot(hidden[0], proj_in, preferred_element_type=jnp.float32)  6.42 us
    all_gather x1, blocking collectives, local(): widened = lax.all_gather(own_docs, 'ffn', axis=1, tiled=True)  3.43 us
    dot_general x1, matrix products, local(): partial_docs = jnp.dot(member, outer, precision=lax.Precision.HIGHEST)  2.65 us
  transfers between devices with their start and end apart: 3, of which 3 were waited for; matrix products, arithmetic and copies ran while one was open for 2% of the time, Pallas kernels for 0%

commit v1 on v0

v1 whole, which is shorter than its diff:
```python
import functools

import jax
import jax.numpy as jnp
from jax import lax
from jax.experimental import pallas as pl
from jax.experimental.pallas import tpu as pltpu
from jax.sharding import PartitionSpec as P

F32 = jnp.float32
BF16 = jnp.bfloat16
MESH = pl.DeviceIdType.MESH
CHUNKS = 4
NT = (((1,), (1,)), ((), ()))
TN = (((0,), (0,)), ((), ()))


def split(x):
    high = x.astype(BF16)
    return high, (x - high.astype(F32)).astype(BF16)


def remote(src, dst, send, recv, **where):
    return pltpu.make_async_remote_copy(
        src_ref=src, dst_ref=dst, send_sem=send, recv_sem=recv,
        device_id=where, device_id_type=MESH,
    )


def docs_kernel(
    S, F, R,
    hid, grads, p_in, p_out, lens,
    right_out, left_out, own_out,
    hbuf, gbuf, pib, pob, opart, ipart, orecv, irecv, a_hi, a_lo, rhs,
    pbuf, prec, vr, vl, vflat, lflat,
    ld_sem, o_send, o_recv, i_send, i_recv, p_send, p_recv,
    v_send, v_recv, b_send, b_recv, l_send, l_recv, m_send, m_recv,
):
    T = gbuf.shape[0]
    rank = pib.shape[1]
    docs = lens.shape[1]
    W = rank // F
    share = docs // S
    cols = W * rank
    trows = rank * rank // S
    q = S // F
    tc = T // CHUNKS
    s = lax.axis_index("seq")
    f = lax.axis_index("ffn")
    r = lax.axis_index("row")
    sib = 1 - r

    def load(src, dst, n):
        c = pltpu.make_async_copy(src, dst, ld_sem.at[n])
        c.start()
        return c

    lo_w = load(p_out, pob, 0)
    lo_x = load(grads.at[0], gbuf, 1)
    li_w = load(p_in, pib, 2)
    li_x = [
        load(hid.at[0, pl.ds(c * tc, tc)], hbuf.at[c], 3 + c) for c in range(CHUNKS)
    ]

    barrier = pltpu.get_barrier_semaphore()
    for ds in range(S):
        for df in range(F):
            if ds or df:
                pl.semaphore_signal(
                    barrier, inc=1,
                    device_id={"seq": lax.rem(s + ds, S), "ffn": lax.rem(f + df, F)},
                    device_id_type=MESH,
                )
    pl.semaphore_signal(barrier, inc=1, device_id={"row": sib}, device_id_type=MESH)

    row = lens[...].astype(F32)
    k_at = lax.broadcasted_iota(jnp.int32, (docs, docs), 0)
    m_at = lax.broadcasted_iota(jnp.int32, (docs, docs), 1)
    wide = jnp.broadcast_to(row, (docs, docs))
    ends = jnp.sum(jnp.where(m_at <= k_at, wide, 0.0), axis=1, keepdims=True)
    starts = jnp.sum(jnp.where(m_at < k_at, wide, 0.0), axis=1, keepdims=True)
    pos = (s * T + lax.broadcasted_iota(jnp.int32, (docs, T), 1)).astype(F32)
    inside = (pos >= starts) & (pos < ends)
    k_own = lax.broadcasted_iota(jnp.int32, (share, docs), 0) + s * share
    m_own = lax.broadcasted_iota(jnp.int32, (share, docs), 1)
    own_len = jnp.sum(
        jnp.where(m_own == k_own, jnp.broadcast_to(row, (share, docs)), 0.0),
        axis=1, keepdims=True,
    )
    own_scale = lax.rsqrt(own_len)

    waits = []
    lo_w.wait()
    lo_x.wait()
    o_here = jnp.dot(gbuf[...], pob[...], preferred_element_type=F32)
    o_t = o_here.T
    for g in range(F):
        opart[g] = o_t[g * W:(g + 1) * W]
    pl.semaphore_wait(barrier, S * F)
    o_copies = []
    for d in range(1, F):
        to = lax.rem(f + d, F)
        c = remote(opart.at[to], orecv.at[d], o_send.at[d], o_recv.at[d], ffn=to)
        c.start()
        o_copies.append(c)
    li_w.wait()
    i_copies = []
    for n in range(CHUNKS):
        li_x[n].wait()
        ipart[n] = jnp.dot(hbuf[n], pib[...], preferred_element_type=F32).T
        for d in range(1, F):
            c = remote(
                ipart.at[n], irecv.at[d, n], i_send.at[d, n], i_recv.at[d, n],
                ffn=lax.rem(f + d, F),
            )
            c.start()
            i_copies.append(c)

    for c in o_copies:
        c.wait_recv()
    o_sum = opart[f]
    for d in range(1, F):
        o_sum = o_sum + orecv[d]
    for i in range(W):
        masked = jnp.where(inside, o_sum[i:i + 1], 0.0)
        high, low = split(masked)
        a_hi[i * docs:(i + 1) * docs] = high
        a_lo[i * docs:(i + 1) * docs] = low
    for n in range(CHUNKS):
        i_sum = ipart[n]
        for d in range(1, F):
            i_copies[n * (F - 1) + d - 1].wait_recv()
            i_sum = i_sum + irecv[d, n]
        high, low = split(i_sum)
        at = slice(n * tc, (n + 1) * tc)
        rhs[0:rank, at] = high
        rhs[rank:2 * rank, at] = high
        rhs[2 * rank:3 * rank, at] = low
        rhs[3 * rank:4 * rank, at] = low
    big = lax.dot_general(a_hi[...], rhs[...], NT, preferred_element_type=F32)
    small = lax.dot_general(a_lo[...], rhs[:2 * rank], NT, preferred_element_type=F32)
    total = big[:, :2 * rank] + (big[:, 2 * rank:] + small)
    first = lax.broadcasted_iota(jnp.int32, (docs, 2 * rank), 1) < rank
    for p in range(W // 2):
        a = total[2 * p * docs:(2 * p + 1) * docs]
        b = total[(2 * p + 1) * docs:(2 * p + 2) * docs]
        tile = jnp.where(first, a, b)
        for g in range(S):
            pbuf[g, :, 2 * rank * p:2 * rank * (p + 1)] = tile[g * share:(g + 1) * share]

    p_copies = []
    for d in range(1, S):
        to = lax.rem(s + d, S)
        c = remote(pbuf.at[to], prec.at[d], p_send.at[d], p_recv.at[d], seq=to)
        c.start()
        p_copies.append(c)
    acc = pbuf[s]
    for d, c in enumerate(p_copies):
        c.wait_recv()
        acc = acc + prec[d + 1]
    own = acc * own_scale
    own_out[0] = own
    vr[r, s] = own

    v_copies = []
    for d in range(1, S):
        c = remote(
            vr.at[r, s], vr.at[r, s], v_send.at[d], v_recv.at[d],
            seq=lax.rem(s + d, S),
        )
        c.start()
        v_copies.append(c)
    l_copies = []
    for e in range(q):
        for d in range(1, F):
            c = remote(
                vr.at[r, s, :, pl.ds(e * trows, trows)], vl.at[r, s],
                l_send.at[e * (F - 1) + d - 1], l_recv.at[s],
                seq=q * f + e, ffn=lax.rem(f + d, F),
            )
            c.start()
            l_copies.append(c)
    b_copies = []
    for d in range(S):
        at = lax.rem(s + S - d, S)
        if d:
            v_copies[d - 1].wait_recv()
        c = remote(vr.at[r, at], vr.at[r, at], b_send.at[d], b_recv.at[d], row=sib)
        c.start()
        b_copies.append(c)

    need_left = f != s // q

    @pl.when(need_left)
    def _():
        for n in range(S):
            got = remote(
                vl.at[r, n], vl.at[r, n], m_send.at[n], l_recv.at[n], row=sib
            )
            got.wait_recv()
            remote(
                vl.at[r, n], vl.at[r, n], m_send.at[n], m_recv.at[n], row=sib
            ).start()

    for c in b_copies:
        c.wait_recv()
    half = R * S * share
    for a in range(R):
        for n in range(S):
            at = (a * S + n) * share
            vflat[at:at + share] = vr[a, n]
    high, low = split(vflat[...])
    right_out[0:half] = high
    right_out[half:2 * half] = low
    right_out[2 * half:3 * half] = high

    @pl.when(need_left)
    def _():
        for n in range(S):
            remote(
                vl.at[r, n], vl.at[r, n], m_send.at[n], m_recv.at[n], row=sib
            ).wait()
        for a in range(R):
            for n in range(S):
                at = (a * S + n) * share
                lflat[at:at + share] = vl[a, n]

    @pl.when(jnp.logical_not(need_left))
    def _():
        lflat[...] = vflat[:, pl.ds(pl.multiple_of(lax.rem(s, q) * trows, 128), trows)]

    high, low = split(lflat[...] * (1.0 / (R * docs)))
    left_out[0:half] = high
    left_out[half:2 * half] = high
    left_out[2 * half:3 * half] = low

    for c in o_copies + i_copies + p_copies + v_copies + l_copies + b_copies:
        c.wait_send()


def gram_kernel(left, right, own, gram, docs):
    gram[...] = lax.dot_general(left[...], right[...], TN, preferred_element_type=F32)

    @pl.when(pl.program_id(0) == 0)
    def _():
        docs[...] = own[...]


def local(hidden, out_grads, proj_in, proj_out, doc_lengths):
    S, F, R = (lax.axis_size(a) for a in ("seq", "ffn", "row"))
    T, H = hidden.shape[1:]
    D = out_grads.shape[2]
    rank = proj_in.shape[1]
    docs = doc_lengths.shape[1]
    W = rank // F
    share = docs // S
    cols = W * rank
    trows = rank * rank // S
    depth = R * docs
    tc = T // CHUNKS
    q = S // F
    dma = pltpu.SemaphoreType.DMA
    vmem = pl.BlockSpec(memory_space=pltpu.VMEM)
    hbm = pl.BlockSpec(memory_space=pl.ANY)
    right, left, own = pl.pallas_call(
        functools.partial(docs_kernel, S, F, R),
        out_shape=(
            jax.ShapeDtypeStruct((3 * depth, cols), BF16),
            jax.ShapeDtypeStruct((3 * depth, trows), BF16),
            jax.ShapeDtypeStruct((1, share, cols), F32),
        ),
        in_specs=[hbm, hbm, hbm, hbm, vmem],
        out_specs=(vmem, vmem, vmem),
        scratch_shapes=[
            pltpu.VMEM((CHUNKS, tc, H), BF16),
            pltpu.VMEM((T, D), BF16),
            pltpu.VMEM((H, rank), BF16),
            pltpu.VMEM((D, rank), BF16),
            pltpu.VMEM((F, W, T), F32),
            pltpu.VMEM((CHUNKS, rank, tc), F32),
            pltpu.VMEM((F, W, T), F32),
            pltpu.VMEM((F, CHUNKS, rank, tc), F32),
            pltpu.VMEM((W * docs, T), BF16),
            pltpu.VMEM((W * docs, T), BF16),
            pltpu.VMEM((4 * rank, T), BF16),
            pltpu.VMEM((S, share, cols), F32),
            pltpu.VMEM((S, share, cols), F32),
            pltpu.VMEM((R, S, share, cols), F32),
            pltpu.VMEM((R, S, share, trows), F32),
            pltpu.VMEM((depth, cols), F32),
            pltpu.VMEM((depth, trows), F32),
            dma((3 + CHUNKS,)),
            dma((F,)), dma((F,)),
            dma((F, CHUNKS)), dma((F, CHUNKS)),
            dma((S,)), dma((S,)),
            dma((S,)), dma((S,)),
            dma((S,)), dma((S,)),
            dma((q * F,)), dma((S,)),
            dma((S,)), dma((S,)),
        ],
        compiler_params=pltpu.CompilerParams(
            collective_id=0, has_side_effects=True, vmem_limit_bytes=48 << 20,
        ),
        name="docs",
    )(hidden, out_grads, proj_in, proj_out, doc_lengths)
    tm = min(128, trows)
    gram, doc_grads = pl.pallas_call(
        gram_kernel,
        grid=(trows // tm,),
        out_shape=(
            jax.ShapeDtypeStruct((trows, cols), F32),
            jax.ShapeDtypeStruct((1, share, cols), F32),
        ),
        in_specs=[
            pl.BlockSpec((3 * depth, tm), lambda i: (0, i)),
            pl.BlockSpec((3 * depth, cols), lambda i: (0, 0)),
            pl.BlockSpec((1, share, cols), lambda i: (0, 0, 0)),
        ],
        out_specs=(
            pl.BlockSpec((tm, cols), lambda i: (i, 0)),
            pl.BlockSpec((1, share, cols), lambda i: (0, 0, 0)),
        ),
        compiler_params=pltpu.CompilerParams(vmem_limit_bytes=32 << 20),
        name="gram",
    )(left, right, own)
    return (doc_grads, gram)


def solution(mesh):
    placed = (
        P(("groups", "row"), "seq", "ffn"),
        P(("groups", "row"), "seq", "ffn"),
        P("ffn", None),
        P("ffn", None),
        P(("groups", "row"), None),
    )
    return jax.shard_map(
        local,
        mesh=mesh,
        in_specs=placed,
        out_specs=(P(("groups", "row"), "seq", "ffn"), P(("groups", "seq"), "ffn")),
        check_vma=False,
    )
```

time: 127 us -> 34.4 us (0.27)
  waiting for transfers between devices: 65.5 us -> 0 us
  Pallas kernels: 0 us -> 28.2 us
  blocking collectives: 22.2 us -> 0 us
  matrix products: 19.5 us -> 0 us
  between operations: 14.5 us -> 0.66 us
  local copies, waits for them, and re-layouts: 0.95 us -> 5.37 us
  other arithmetic: 4.03 us -> 0 us
    unnamed x4 -> x0, waiting for transfers between devices: 32.5 us -> none
    pallas_call x0 -> x2, Pallas kernels: none -> 28.2 us  [the longest x1 22.6 us: local(): pl.pallas_call(functools.partial(docs_kernel, S, F, R), out_shape=(jax.Sh...]
    all_gather x2 -> x0, blocking collectives: 22.2 us -> none  [the longest x1 18.8 us: local(): piece = lax.all_gather(widened, ('seq', 'row'), axis=0, tiled=True)]
    psum x1 -> x0, waiting for transfers between devices: 20.1 us -> none  [local(): input_proj = lax.psum(input_part, 'ffn')]
    dot_general x4 -> x0, matrix products: 19.5 us -> none  [the longest x1 9.01 us: local(): jnp.einsum('dk,dl->kl', left_part, right_part, precision=lax.Precision.HI...]
    reduce_scatter x1 -> x0, waiting for transfers between devices: 12.9 us -> none  [local(): lax.psum_scatter(output_part, 'ffn', scatter_dimension=1, tiled=True)]
    unnamed x10 -> x6, local copies, waits for them, and re-layouts: 0.79 us -> 5.37 us
    mul x2 -> x0, other arithmetic: 2.34 us -> none  [the longest x1 1.43 us: local(): output_piece[:, :, None] * input_proj[:, None, :]]
  transfers between devices with their start and end apart: 3 -> 0, of which waited for: 3 -> 0; matrix products, arithmetic and copies ran while one was open for 2% -> 0% of each run, Pallas kernels for 0% -> 0%
where the time goes in v1:
time: 34.4 us; the launch traced here: 34.2 us
  Pallas kernels  28.2 us (82%)
  local copies, waits for them, and re-layouts  5.37 us (16%)
  between operations  0.66 us (2%)
    pallas_call x1, Pallas kernels, local(): pl.pallas_call(functools.partial(docs_kernel, S, F, R), out_shape=(jax.Sh...  22.6 us
    pallas_call x1, Pallas kernels, local(): pl.pallas_call(gram_kernel, grid=(trows // tm,), out_shape=(jax.ShapeDtyp...  5.57 us
    unnamed x6, local copies, waits for them, and re-layouts  5.37 us

profile of v1, /device:TPU:1, one launch (start us, length us, event | category | flops | bytes accessed | tf_op | source)
XLA Modules:
  0.0 34.2 jit_solution(7253594990319432989)
XLA Ops:
  0.6 1.2 %copy.8.p_out = bf16[2048,64]{1,0:T(8,128)(2,1)S(1)} copy(bf16[2048,64]{0,1:T(8,128)(2,1)} %param.8) | data formatting | bytes 524288 | tf_op args[3]
  1.9 1.9 %copy.7.p_in = bf16[7168,64]{1,0:T(8,128)(2,1)S(1)} copy(bf16[7168,64]{0,1:T(8,128)(2,1)} %param.7) | data formatting | bytes 1835008 | tf_op args[2]
  3.8 0.0 copy-start
  3.8 1.6 %copy-done = bf16[1,512,2048]{2,1,0:T(8,128)(2,1)S(1)} copy-done((bf16[1,512,2048]{2,1,0:T(8,128)(2,1)S(1)}, bf16[1,512,2048]{2,1,0:T(8,128)(2,1)}, u32[]{:S(2)}) %copy-start) | copy-done | bytes 2097176
  5.4 0.0 copy-start.1
  5.4 0.7 %copy-done.1 = s32[1,16]{1,0:T(1,128)S(1)} copy-done((s32[1,16]{1,0:T(1,128)S(1)}, s32[1,16]{1,0:T(1,128)}, u32[]{:S(2)}) %copy-start.1) | copy-done | bytes 88
  6.0 22.6 %docs.1 = (bf16[96,2048]{1,0:T(8,128)(2,1)S(1)}, bf16[96,1024]{1,0:T(8,128)(2,1)S(1)}, f32[1,4,2048]{2,1,0:T(4,128)S(1)}) custom-call(bf16[1,512,7168]{2,1,0:T(8,128)(2,1)} %hid.1, bf16[1,512,2048]{2,1,0:T(8,128)(2,1)S(1)} %copy-done, bf16[7168,64]{1,0:T(8,128)(2,1)S(1)} %copy.7.p_in, bf16[2048,64]{1,0:T(8,128)(2,1)S(1)} %copy.8.p_out, s32[1,16]{1,0:T(1,128)S(1)} %copy-done.1), custom_call_target="tpu_custom_call" | custom-call | tf_op jit(solution)/shard_map/docs/pallas_call | solution.py:265
  28.7 5.6 %gram.1 = (f32[1024,2048]{1,0:T(8,128)}, f32[1,4,2048]{2,1,0:T(4,128)}) custom-call(bf16[96,1024]{1,0:T(8,128)(2,1)S(1)} %get-tuple-element.7.left, bf16[96,2048]{1,0:T(8,128)(2,1)S(1)} %get-tuple-element.8.right, f32[1,4,2048]{2,1,0:T(4,128)S(1)} %get-tuple-element.9.own), custom_call_target="tpu_custom_call" | custom-call | tf_op jit(solution)/shard_map/gram/pallas_call | solution.py:307
Async XLA Ops:
  3.8 1.6 %copy-start = (bf16[1,512,2048]{2,1,0:T(8,128)(2,1)S(1)}, bf16[1,512,2048]{2,1,0:T(8,128)(2,1)}, u32[]{:S(2)}) copy-start(bf16[1,512,2048]{2,1,0:T(8,128)(2,1)} %grads.1) | copy-start | bytes 6291460
  5.4 0.7 %copy-start.1 = (s32[1,16]{1,0:T(1,128)S(1)}, s32[1,16]{1,0:T(1,128)}, u32[]{:S(2)}) copy-start(s32[1,16]{1,0:T(1,128)} %lens.1) | copy-start | bytes 196

commit v2 on v1

--- a/solution.py
+++ b/solution.py
@@ -37,7 +37,7 @@
     v_send, v_recv, b_send, b_recv, l_send, l_recv, m_send, m_recv,
 ):
     T = gbuf.shape[0]
-    rank = pib.shape[1]
+    rank = pib.shape[0]
     docs = lens.shape[1]
     W = rank // F
     share = docs // S
@@ -92,7 +92,7 @@
     waits = []
     lo_w.wait()
     lo_x.wait()
-    o_here = jnp.dot(gbuf[...], pob[...], preferred_element_type=F32)
+    o_here = lax.dot_general(gbuf[...], pob[...], NT, preferred_element_type=F32)
     o_t = o_here.T
     for g in range(F):
         opart[g] = o_t[g * W:(g + 1) * W]
@@ -107,7 +107,7 @@
     i_copies = []
     for n in range(CHUNKS):
         li_x[n].wait()
-        ipart[n] = jnp.dot(hbuf[n], pib[...], preferred_element_type=F32).T
+        ipart[n] = lax.dot_general(hbuf[n], pib[...], NT, preferred_element_type=F32).T
         for d in range(1, F):
             c = remote(
                 ipart.at[n], irecv.at[d, n], i_send.at[d, n], i_recv.at[d, n],
@@ -137,82 +137,91 @@
         rhs[rank:2 * rank, at] = high
         rhs[2 * rank:3 * rank, at] = low
         rhs[3 * rank:4 * rank, at] = low
-    big = lax.dot_general(a_hi[...], rhs[...], NT, preferred_element_type=F32)
-    small = lax.dot_general(a_lo[...], rhs[:2 * rank], NT, preferred_element_type=F32)
-    total = big[:, :2 * rank] + (big[:, 2 * rank:] + small)
     first = lax.broadcasted_iota(jnp.int32, (docs, 2 * rank), 1) < rank
-    for p in range(W // 2):
-        a = total[2 * p * docs:(2 * p + 1) * docs]
-        b = total[(2 * p + 1) * docs:(2 * p + 2) * docs]
-        tile = jnp.where(first, a, b)
-        for g in range(S):
-            pbuf[g, :, 2 * rank * p:2 * rank * (p + 1)] = tile[g * share:(g + 1) * share]
-
+    pairs = W // (2 * q)
     p_copies = []
-    for d in range(1, S):
-        to = lax.rem(s + d, S)
-        c = remote(pbuf.at[to], prec.at[d], p_send.at[d], p_recv.at[d], seq=to)
-        c.start()
-        p_copies.append(c)
-    acc = pbuf[s]
-    for d, c in enumerate(p_copies):
-        c.wait_recv()
-        acc = acc + prec[d + 1]
-    own = acc * own_scale
-    own_out[0] = own
-    vr[r, s] = own
+    for p in range(q):
+        at = slice(2 * pairs * docs * p, 2 * pairs * docs * (p + 1))
+        big = lax.dot_general(a_hi[at], rhs[...], NT, preferred_element_type=F32)
+        small = lax.dot_general(a_lo[at], rhs[:2 * rank], NT, preferred_element_type=F32)
+        total = big[:, :2 * rank] + (big[:, 2 * rank:] + small)
+        for u in range(pairs):
+            a = total[2 * u * docs:(2 * u + 1) * docs]
+            b = total[(2 * u + 1) * docs:(2 * u + 2) * docs]
+            tile = jnp.where(first, a, b)
+            for g in range(S):
+                pbuf[p, g, :, 2 * rank * u:2 * rank * (u + 1)] = tile[g * share:(g + 1) * share]
+        for d in range(1, S):
+            to = lax.rem(s + d, S)
+            c = remote(pbuf.at[p, to], prec.at[p, d], p_send.at[p, d], p_recv.at[p, d], seq=to)
+            c.start()
+            p_copies.append(c)
 
     v_copies = []
-    for d in range(1, S):
+    l_copies = []
+    b_copies = []
+
+    def relay(p, d):
+        at = lax.rem(s + S - d, S)
         c = remote(
-            vr.at[r, s], vr.at[r, s], v_send.at[d], v_recv.at[d],
-            seq=lax.rem(s + d, S),
+            vr.at[p, r, at], vr.at[p, r, at], b_send.at[p, d], b_recv.at[p, d], row=sib
         )
         c.start()
-        v_copies.append(c)
-    l_copies = []
-    for e in range(q):
+        b_copies.append(c)
+
+    for p in range(q):
+        acc = pbuf[p, s]
+        for d in range(1, S):
+            p_copies[p * (S - 1) + d - 1].wait_recv()
+            acc = acc + prec[p, d]
+        own = acc * own_scale
+        own_out[0, :, p * trows:(p + 1) * trows] = own
+        vr[p, r, s] = own
+        for d in range(1, S):
+            c = remote(
+                vr.at[p, r, s], vr.at[p, r, s], v_send.at[p, d], v_recv.at[p, d],
+                seq=lax.rem(s + d, S),
+            )
+            c.start()
+            v_copies.append(c)
         for d in range(1, F):
             c = remote(
-                vr.at[r, s, :, pl.ds(e * trows, trows)], vl.at[r, s],
-                l_send.at[e * (F - 1) + d - 1], l_recv.at[s],
-                seq=q * f + e, ffn=lax.rem(f + d, F),
+                vr.at[p, r, s], vl.at[r, s], l_send.at[p, d], l_recv.at[s],
+                seq=q * f + p, ffn=lax.rem(f + d, F),
             )
             c.start()
             l_copies.append(c)
-    b_copies = []
-    for d in range(S):
-        at = lax.rem(s + S - d, S)
-        if d:
-            v_copies[d - 1].wait_recv()
-        c = remote(vr.at[r, at], vr.at[r, at], b_send.at[d], b_recv.at[d], row=sib)
-        c.start()
-        b_copies.append(c)
+        relay(p, 0)
+    for p in range(q):
+        for d in range(1, S):
+            v_copies[p * (S - 1) + d - 1].wait_recv()
+            relay(p, d)
 
     need_left = f != s // q
 
     @pl.when(need_left)
     def _():
         for n in range(S):
-            got = remote(
+            remote(
                 vl.at[r, n], vl.at[r, n], m_send.at[n], l_recv.at[n], row=sib
-            )
-            got.wait_recv()
+            ).wait_recv()
             remote(
                 vl.at[r, n], vl.at[r, n], m_send.at[n], m_recv.at[n], row=sib
             ).start()
 
-    for c in b_copies:
-        c.wait_recv()
-    half = R * S * share
-    for a in range(R):
-        for n in range(S):
-            at = (a * S + n) * share
-            vflat[at:at + share] = vr[a, n]
-    high, low = split(vflat[...])
-    right_out[0:half] = high
-    right_out[half:2 * half] = low
-    right_out[2 * half:3 * half] = high
+    depth = R * S * share
+    for p in range(q):
+        for c in b_copies[p:p + 1] + b_copies[q + p * (S - 1):q + (p + 1) * (S - 1)]:
+            c.wait_recv()
+        for a in range(R):
+            for n in range(S):
+                at = (a * S + n) * share
+                vflat[p, at:at + share] = vr[p, a, n]
+        high, low = split(vflat[p])
+        at = slice(p * trows, (p + 1) * trows)
+        right_out[0:depth, at] = high
+        right_out[depth:2 * depth, at] = low
+        right_out[2 * depth:3 * depth, at] = high
 
     @pl.when(need_left)
     def _():
@@ -227,23 +236,33 @@
 
     @pl.when(jnp.logical_not(need_left))
     def _():
-        lflat[...] = vflat[:, pl.ds(pl.multiple_of(lax.rem(s, q) * trows, 128), trows)]
+        lflat[...] = vflat[lax.rem(s, q)]
 
     high, low = split(lflat[...] * (1.0 / (R * docs)))
-    left_out[0:half] = high
-    left_out[half:2 * half] = high
-    left_out[2 * half:3 * half] = low
+    left_out[0:depth] = high
+    left_out[depth:2 * depth] = high
+    left_out[2 * depth:3 * depth] = low
 
     for c in o_copies + i_copies + p_copies + v_copies + l_copies + b_copies:
         c.wait_send()
 
 
-def gram_kernel(left, right, own, gram, docs):
-    gram[...] = lax.dot_general(left[...], right[...], TN, preferred_element_type=F32)
-
-    @pl.when(pl.program_id(0) == 0)
-    def _():
-        docs[...] = own[...]
+def gram_kernel(left, right, own, gram, docs, tiles, sem, own_sem):
+    own_copy = pltpu.make_async_copy(own, docs, own_sem)
+    own_copy.start()
+    rows = left[...].T
+    copies = []
+    for n in range(tiles.shape[0]):
+        tm = tiles.shape[1]
+        tiles[n] = jnp.dot(
+            rows[n * tm:(n + 1) * tm], right[...], preferred_element_type=F32
+        )
+        c = pltpu.make_async_copy(tiles.at[n], gram.at[pl.ds(n * tm, tm)], sem.at[n])
+        c.start()
+        copies.append(c)
+    for c in copies:
+        c.wait()
+    own_copy.wait()
 
 
 def local(hidden, out_grads, proj_in, proj_out, doc_lengths):
@@ -261,21 +280,21 @@
     q = S // F
     dma = pltpu.SemaphoreType.DMA
     vmem = pl.BlockSpec(memory_space=pltpu.VMEM)
-    hbm = pl.BlockSpec(memory_space=pl.ANY)
+    hbm = pl.BlockSpec(memory_space=pltpu.HBM)
     right, left, own = pl.pallas_call(
         functools.partial(docs_kernel, S, F, R),
         out_shape=(
-            jax.ShapeDtypeStruct((3 * depth, cols), BF16),
-            jax.ShapeDtypeStruct((3 * depth, trows), BF16),
-            jax.ShapeDtypeStruct((1, share, cols), F32),
+            pltpu.VMEM((3 * depth, cols), BF16),
+            pltpu.VMEM((3 * depth, trows), BF16),
+            pltpu.VMEM((1, share, cols), F32),
         ),
         in_specs=[hbm, hbm, hbm, hbm, vmem],
         out_specs=(vmem, vmem, vmem),
         scratch_shapes=[
             pltpu.VMEM((CHUNKS, tc, H), BF16),
             pltpu.VMEM((T, D), BF16),
-            pltpu.VMEM((H, rank), BF16),
-            pltpu.VMEM((D, rank), BF16),
+            pltpu.VMEM((rank, H), BF16),
+            pltpu.VMEM((rank, D), BF16),
             pltpu.VMEM((F, W, T), F32),
             pltpu.VMEM((CHUNKS, rank, tc), F32),
             pltpu.VMEM((F, W, T), F32),
@@ -283,44 +302,39 @@
             pltpu.VMEM((W * docs, T), BF16),
             pltpu.VMEM((W * docs, T), BF16),
             pltpu.VMEM((4 * rank, T), BF16),
-            pltpu.VMEM((S, share, cols), F32),
-            pltpu.VMEM((S, share, cols), F32),
-            pltpu.VMEM((R, S, share, cols), F32),
+            pltpu.VMEM((q, S, share, trows), F32),
+            pltpu.VMEM((q, S, share, trows), F32),
+            pltpu.VMEM((q, R, S, share, trows), F32),
             pltpu.VMEM((R, S, share, trows), F32),
-            pltpu.VMEM((depth, cols), F32),
+            pltpu.VMEM((q, depth, trows), F32),
             pltpu.VMEM((depth, trows), F32),
             dma((3 + CHUNKS,)),
             dma((F,)), dma((F,)),
             dma((F, CHUNKS)), dma((F, CHUNKS)),
-            dma((S,)), dma((S,)),
-            dma((S,)), dma((S,)),
-            dma((S,)), dma((S,)),
-            dma((q * F,)), dma((S,)),
+            dma((q, S)), dma((q, S)),
+            dma((q, S)), dma((q, S)),
+            dma((q, S)), dma((q, S)),
+            dma((q, F)), dma((S,)),
             dma((S,)), dma((S,)),
         ],
         compiler_params=pltpu.CompilerParams(
-            collective_id=0, has_side_effects=True, vmem_limit_bytes=48 << 20,
+            collective_id=0, has_side_effects=True, vmem_limit_bytes=60 << 20,
         ),
         name="docs",
-    )(hidden, out_grads, proj_in, proj_out, doc_lengths)
+    )(hidden, out_grads, proj_in.T, proj_out.T, doc_lengths)
     tm = min(128, trows)
     gram, doc_grads = pl.pallas_call(
         gram_kernel,
-        grid=(trows // tm,),
         out_shape=(
             jax.ShapeDtypeStruct((trows, cols), F32),
             jax.ShapeDtypeStruct((1, share, cols), F32),
         ),
-        in_specs=[
-            pl.BlockSpec((3 * depth, tm), lambda i: (0, i)),
-            pl.BlockSpec((3 * depth, cols), lambda i: (0, 0)),
-            pl.BlockSpec((1, share, cols), lambda i: (0, 0, 0)),
+        in_specs=[vmem, vmem, vmem],
+        out_specs=(hbm, hbm),
+        scratch_shapes=[
+            pltpu.VMEM((trows // tm, tm, cols), F32), dma((trows // tm,)), dma,
         ],
-        out_specs=(
-            pl.BlockSpec((tm, cols), lambda i: (i, 0)),
-            pl.BlockSpec((1, share, cols), lambda i: (0, 0, 0)),
-        ),
-        compiler_params=pltpu.CompilerParams(vmem_limit_bytes=32 << 20),
+        compiler_params=pltpu.CompilerParams(vmem_limit_bytes=44 << 20),
         name="gram",
     )(left, right, own)
     return (doc_grads, gram)

time: 34.4 us -> 29.2 us (0.85)
  local copies, waits for them, and re-layouts: 5.37 us -> 0 us
    unnamed x6 -> x0, local copies, waits for them, and re-layouts: 5.37 us -> none
where the time goes in v2:
time: 29.2 us; the launch traced here: 29.1 us
  Pallas kernels  28.4 us (97%)
  between operations  0.64 us (2%)
    pallas_call x1, Pallas kernels, local(): pl.pallas_call(functools.partial(docs_kernel, S, F, R), out_shape=(pltpu....  24.7 us
    pallas_call x1, Pallas kernels, local(): pl.pallas_call(gram_kernel, out_shape=(jax.ShapeDtypeStruct((trows, cols)...  3.71 us

profile of v2, /device:TPU:1, one launch (start us, length us, event | category | flops | bytes accessed | tf_op | source)
XLA Modules:
  0.0 29.1 jit_solution(5819002636587831302)
XLA Ops:
  0.6 24.7 %docs.1 = (bf16[96,2048]{1,0:T(8,128)(2,1)S(1)}, bf16[96,1024]{1,0:T(8,128)(2,1)S(1)}, f32[1,4,2048]{2,1,0:T(4,128)S(1)}) custom-call(bf16[1,512,7168]{2,1,0:T(8,128)(2,1)} %hid.1, bf16[1,512,2048]{2,1,0:T(8,128)(2,1)} %grads.1, bf16[64,7168]{1,0:T(8,128)(2,1)} %bitcast.2, bf16[64,2048]{1,0:T(8,128)(2,1)} %bitcast.3, s32[1,16]{1,0:T(1,128)} %lens.1), custom_call_target="tpu_custom_call" | custom-call | tf_op jit(solution)/shard_map/docs/pallas_call | solution.py:284
  25.3 3.7 %gram.1 = (f32[1024,2048]{1,0:T(8,128)}, f32[1,4,2048]{2,1,0:T(4,128)}) custom-call(bf16[96,1024]{1,0:T(8,128)(2,1)S(1)} %get-tuple-element.7.left, bf16[96,2048]{1,0:T(8,128)(2,1)S(1)} %get-tuple-element.8.right, f32[1,4,2048]{2,1,0:T(4,128)S(1)} %get-tuple-element.9.own), custom_call_target="tpu_custom_call" | custom-call | tf_op jit(solution)/shard_map/gram/pallas_call | solution.py:326

commit v3 on v2

--- a/solution.py
+++ b/solution.py
@@ -29,9 +29,9 @@
 
 def docs_kernel(
     S, F, R,
-    hid, grads, p_in, p_out, lens,
+    hid, grads, p_in, p_out, lens_hbm,
     right_out, left_out, own_out,
-    hbuf, gbuf, pib, pob, opart, ipart, orecv, irecv, a_hi, a_lo, rhs,
+    lens, hbuf, gbuf, pib, pob, opart, ipart, orecv, irecv, a_hi, a_lo, rhs,
     pbuf, prec, vr, vl, vflat, lflat,
     ld_sem, o_send, o_recv, i_send, i_recv, p_send, p_recv,
     v_send, v_recv, b_send, b_recv, l_send, l_recv, m_send, m_recv,
@@ -62,6 +62,8 @@
         load(hid.at[0, pl.ds(c * tc, tc)], hbuf.at[c], 3 + c) for c in range(CHUNKS)
     ]
 
+    lens_x = load(lens_hbm, lens, 3 + CHUNKS)
+
     barrier = pltpu.get_barrier_semaphore()
     for ds in range(S):
         for df in range(F):
@@ -73,23 +75,6 @@
                 )
     pl.semaphore_signal(barrier, inc=1, device_id={"row": sib}, device_id_type=MESH)
 
-    row = lens[...].astype(F32)
-    k_at = lax.broadcasted_iota(jnp.int32, (docs, docs), 0)
-    m_at = lax.broadcasted_iota(jnp.int32, (docs, docs), 1)
-    wide = jnp.broadcast_to(row, (docs, docs))
-    ends = jnp.sum(jnp.where(m_at <= k_at, wide, 0.0), axis=1, keepdims=True)
-    starts = jnp.sum(jnp.where(m_at < k_at, wide, 0.0), axis=1, keepdims=True)
-    pos = (s * T + lax.broadcasted_iota(jnp.int32, (docs, T), 1)).astype(F32)
-    inside = (pos >= starts) & (pos < ends)
-    k_own = lax.broadcasted_iota(jnp.int32, (share, docs), 0) + s * share
-    m_own = lax.broadcasted_iota(jnp.int32, (share, docs), 1)
-    own_len = jnp.sum(
-        jnp.where(m_own == k_own, jnp.broadcast_to(row, (share, docs)), 0.0),
-        axis=1, keepdims=True,
-    )
-    own_scale = lax.rsqrt(own_len)
-
-    waits = []
     lo_w.wait()
     lo_x.wait()
     o_here = lax.dot_general(gbuf[...], pob[...], NT, preferred_element_type=F32)
@@ -115,6 +100,23 @@
             )
             c.start()
             i_copies.append(c)
+
+    lens_x.wait()
+    row = lens[...].astype(F32)
+    k_at = lax.broadcasted_iota(jnp.int32, (docs, docs), 0)
+    m_at = lax.broadcasted_iota(jnp.int32, (docs, docs), 1)
+    wide = jnp.broadcast_to(row, (docs, docs))
+    ends = jnp.sum(jnp.where(m_at <= k_at, wide, 0.0), axis=1, keepdims=True)
+    starts = jnp.sum(jnp.where(m_at < k_at, wide, 0.0), axis=1, keepdims=True)
+    pos = (s * T + lax.broadcasted_iota(jnp.int32, (docs, T), 1)).astype(F32)
+    inside = (pos >= starts) & (pos < ends)
+    k_own = lax.broadcasted_iota(jnp.int32, (share, docs), 0) + s * share
+    m_own = lax.broadcasted_iota(jnp.int32, (share, docs), 1)
+    own_len = jnp.sum(
+        jnp.where(m_own == k_own, jnp.broadcast_to(row, (share, docs)), 0.0),
+        axis=1, keepdims=True,
+    )
+    own_scale = lax.rsqrt(own_len)
 
     for c in o_copies:
         c.wait_recv()
@@ -288,9 +290,10 @@
             pltpu.VMEM((3 * depth, trows), BF16),
             pltpu.VMEM((1, share, cols), F32),
         ),
-        in_specs=[hbm, hbm, hbm, hbm, vmem],
+        in_specs=[hbm] * 5,
         out_specs=(vmem, vmem, vmem),
         scratch_shapes=[
+            pltpu.VMEM((1, docs), jnp.int32),
             pltpu.VMEM((CHUNKS, tc, H), BF16),
             pltpu.VMEM((T, D), BF16),
             pltpu.VMEM((rank, H), BF16),
@@ -308,7 +311,7 @@
             pltpu.VMEM((R, S, share, trows), F32),
             pltpu.VMEM((q, depth, trows), F32),
             pltpu.VMEM((depth, trows), F32),
-            dma((3 + CHUNKS,)),
+            dma((4 + CHUNKS,)),
             dma((F,)), dma((F,)),
             dma((F, CHUNKS)), dma((F, CHUNKS)),
             dma((q, S)), dma((q, S)),

time: 29.2 us -> 28.5 us (0.976)
  Pallas kernels: 28.4 us -> 27.8 us
    pallas_call x1, Pallas kernels: 24.7 us -> 24.1 us  [local(): pl.pallas_call(functools.partial(docs_kernel, S, F, R), out_shape=(pltpu....]
where the time goes in v3:
time: 28.5 us; the launch traced here: 28.4 us
  Pallas kernels  27.8 us (98%)
  between operations  0.64 us (2%)
    pallas_call x1, Pallas kernels, local(): pl.pallas_call(functools.partial(docs_kernel, S, F, R), out_shape=(pltpu....  24.1 us
    pallas_call x1, Pallas kernels, local(): pl.pallas_call(gram_kernel, out_shape=(jax.ShapeDtypeStruct((trows, cols)...  3.71 us

profile of v3, /device:TPU:1, one launch (start us, length us, event | category | flops | bytes accessed | tf_op | source)
XLA Modules:
  0.0 28.4 jit_solution(4745270922544752132)
XLA Ops:
  0.6 24.1 %docs.1 = (bf16[96,2048]{1,0:T(8,128)(2,1)S(1)}, bf16[96,1024]{1,0:T(8,128)(2,1)S(1)}, f32[1,4,2048]{2,1,0:T(4,128)S(1)}) custom-call(bf16[1,512,7168]{2,1,0:T(8,128)(2,1)} %hid.1, bf16[1,512,2048]{2,1,0:T(8,128)(2,1)} %grads.1, bf16[64,7168]{1,0:T(8,128)(2,1)} %bitcast.2, bf16[64,2048]{1,0:T(8,128)(2,1)} %bitcast.3, s32[1,16]{1,0:T(1,128)} %lens_hbm.1), custom_call_target="tpu_custom_call" | custom-call | tf_op jit(solution)/shard_map/docs/pallas_call | solution.py:286
  24.7 3.7 %gram.1 = (f32[1024,2048]{1,0:T(8,128)}, f32[1,4,2048]{2,1,0:T(4,128)}) custom-call(bf16[96,1024]{1,0:T(8,128)(2,1)S(1)} %get-tuple-element.7.left, bf16[96,2048]{1,0:T(8,128)(2,1)S(1)} %get-tuple-element.8.right, f32[1,4,2048]{2,1,0:T(4,128)S(1)} %get-tuple-element.9.own), custom_call_target="tpu_custom_call" | custom-call | tf_op jit(solution)/shard_map/gram/pallas_call | solution.py:329

commit v4 on v3

--- a/solution.py
+++ b/solution.py
@@ -15,6 +15,10 @@
 TN = (((0,), (0,)), ((), ()))
 
 
+def ORDER(n):
+    return sorted(range(1, n), key=lambda d: -min(d, n - d))
+
+
 def split(x):
     high = x.astype(BF16)
     return high, (x - high.astype(F32)).astype(BF16)
@@ -32,7 +36,7 @@
     hid, grads, p_in, p_out, lens_hbm,
     right_out, left_out, own_out,
     lens, hbuf, gbuf, pib, pob, opart, ipart, orecv, irecv, a_hi, a_lo, rhs,
-    pbuf, prec, vr, vl, vflat, lflat,
+    begun, pbuf, prec, vr, vl, vflat, lflat,
     ld_sem, o_send, o_recv, i_send, i_recv, p_send, p_recv,
     v_send, v_recv, b_send, b_recv, l_send, l_recv, m_send, m_recv,
 ):
@@ -128,7 +132,23 @@
         high, low = split(masked)
         a_hi[i * docs:(i + 1) * docs] = high
         a_lo[i * docs:(i + 1) * docs] = low
+    pairs = W // (2 * q)
+    early = (CHUNKS - 1) * tc
+
+    def product(p, lo, hi):
+        at = slice(2 * pairs * docs * p, 2 * pairs * docs * (p + 1))
+        big = lax.dot_general(
+            a_hi[at, lo:hi], rhs[:, lo:hi], NT, preferred_element_type=F32
+        )
+        small = lax.dot_general(
+            a_lo[at, lo:hi], rhs[:2 * rank, lo:hi], NT, preferred_element_type=F32
+        )
+        return big[:, :2 * rank] + (big[:, 2 * rank:] + small)
+
     for n in range(CHUNKS):
+        if n == CHUNKS - 1:
+            for p in range(q):
+                begun[p] = product(p, 0, early)
         i_sum = ipart[n]
         for d in range(1, F):
             i_copies[n * (F - 1) + d - 1].wait_recv()
@@ -140,20 +160,16 @@
         rhs[2 * rank:3 * rank, at] = low
         rhs[3 * rank:4 * rank, at] = low
     first = lax.broadcasted_iota(jnp.int32, (docs, 2 * rank), 1) < rank
-    pairs = W // (2 * q)
     p_copies = []
     for p in range(q):
-        at = slice(2 * pairs * docs * p, 2 * pairs * docs * (p + 1))
-        big = lax.dot_general(a_hi[at], rhs[...], NT, preferred_element_type=F32)
-        small = lax.dot_general(a_lo[at], rhs[:2 * rank], NT, preferred_element_type=F32)
-        total = big[:, :2 * rank] + (big[:, 2 * rank:] + small)
+        total = begun[p] + product(p, early, T)
         for u in range(pairs):
             a = total[2 * u * docs:(2 * u + 1) * docs]
             b = total[(2 * u + 1) * docs:(2 * u + 2) * docs]
             tile = jnp.where(first, a, b)
             for g in range(S):
                 pbuf[p, g, :, 2 * rank * u:2 * rank * (u + 1)] = tile[g * share:(g + 1) * share]
-        for d in range(1, S):
+        for d in ORDER(S):
             to = lax.rem(s + d, S)
             c = remote(pbuf.at[p, to], prec.at[p, d], p_send.at[p, d], p_recv.at[p, d], seq=to)
             c.start()
@@ -174,12 +190,12 @@
     for p in range(q):
         acc = pbuf[p, s]
         for d in range(1, S):
-            p_copies[p * (S - 1) + d - 1].wait_recv()
+            p_copies[p * (S - 1) + ORDER(S).index(d)].wait_recv()
             acc = acc + prec[p, d]
         own = acc * own_scale
         own_out[0, :, p * trows:(p + 1) * trows] = own
         vr[p, r, s] = own
-        for d in range(1, S):
+        for d in ORDER(S):
             c = remote(
                 vr.at[p, r, s], vr.at[p, r, s], v_send.at[p, d], v_recv.at[p, d],
                 seq=lax.rem(s + d, S),
@@ -195,8 +211,8 @@
             l_copies.append(c)
         relay(p, 0)
     for p in range(q):
-        for d in range(1, S):
-            v_copies[p * (S - 1) + d - 1].wait_recv()
+        for d in reversed(ORDER(S)):
+            v_copies[p * (S - 1) + ORDER(S).index(d)].wait_recv()
             relay(p, d)
 
     need_left = f != s // q
@@ -305,6 +321,7 @@
             pltpu.VMEM((W * docs, T), BF16),
             pltpu.VMEM((W * docs, T), BF16),
             pltpu.VMEM((4 * rank, T), BF16),
+            pltpu.VMEM((q, W * docs // q, 2 * rank), F32),
             pltpu.VMEM((q, S, share, trows), F32),
             pltpu.VMEM((q, S, share, trows), F32),
             pltpu.VMEM((q, R, S, share, trows), F32),

time: 28.5 us -> 28.4 us (level)
  no operation moved by 1% of the time
where the time goes in v4:
time: 28.4 us; the launch traced here: 28.3 us
  Pallas kernels  27.6 us (97%)
  between operations  0.64 us (2%)
    pallas_call x1, Pallas kernels, local(): pl.pallas_call(functools.partial(docs_kernel, S, F, R), out_shape=(pltpu....  23.9 us
    pallas_call x1, Pallas kernels, local(): pl.pallas_call(gram_kernel, out_shape=(jax.ShapeDtypeStruct((trows, cols)...  3.71 us

profile of v4, /device:TPU:1, one launch (start us, length us, event | category | flops | bytes accessed | tf_op | source)
XLA Modules:
  0.0 28.3 jit_solution(7244955702581231200)
XLA Ops:
  0.6 23.9 %docs.1 = (bf16[96,2048]{1,0:T(8,128)(2,1)S(1)}, bf16[96,1024]{1,0:T(8,128)(2,1)S(1)}, f32[1,4,2048]{2,1,0:T(4,128)S(1)}) custom-call(bf16[1,512,7168]{2,1,0:T(8,128)(2,1)} %hid.1, bf16[1,512,2048]{2,1,0:T(8,128)(2,1)} %grads.1, bf16[64,7168]{1,0:T(8,128)(2,1)} %bitcast.2, bf16[64,2048]{1,0:T(8,128)(2,1)} %bitcast.3, s32[1,16]{1,0:T(1,128)} %lens_hbm.1), custom_call_target="tpu_custom_call" | custom-call | tf_op jit(solution)/shard_map/docs/pallas_call | solution.py:302
  24.6 3.7 %gram.1 = (f32[1024,2048]{1,0:T(8,128)}, f32[1,4,2048]{2,1,0:T(4,128)}) custom-call(bf16[96,1024]{1,0:T(8,128)(2,1)S(1)} %get-tuple-element.7.left, bf16[96,2048]{1,0:T(8,128)(2,1)S(1)} %get-tuple-element.8.right, f32[1,4,2048]{2,1,0:T(4,128)S(1)} %get-tuple-element.9.own), custom_call_target="tpu_custom_call" | custom-call | tf_op jit(solution)/shard_map/gram/pallas_call | solution.py:346
